TPU v7x, 256 devices: a whole 4x4x8 slice. The times are simulated.
256 devices in a mesh: lev: 8 (over x_lo, y), tile: 32 (over x_hi, z, core).
Axes of the slice: x: 4 (x_hi: 2, x_lo: 2; x = x_hi * 2 + x_lo), y: 4, z: 8, core: 2. Of those that a mesh axis runs over, the one named last changes fastest.
Arguments:
- cotangent: bfloat16 [72, 96, 32768], P('lev', None, 'tile'), may hold values from -6 to 6
- particles: bfloat16 [72, 96, 32768], P('lev', None, 'tile'), may hold values from 0.049804688 to 2
- coag_rate: float32 [72], P('lev'), may hold values from 0.004 to 0.015
- courant: float32 [2, 72, 32768], P(None, 'lev', 'tile'), may hold values from 0.05 to 0.45
- offsets: int32 [2, 32768], P(None, 'tile'), may hold values from -2 to 2
- mass_flux: bfloat16 [72, 72, 32768], P(None, None, ('tile', 'lev')), may hold values from -0.75 to 0.75
- cloud_top: int32 [32768], P(('tile', 'lev')), may hold values from 18 to 71
Outputs:
- result: float32 [72, 96, 32768], P(None, None, ('tile', 'lev'))
All inputs are finite; a program needn't handle non-finite values.
Results may differ from a plain program's by a relative error of at most 0.0029.
Values may be sent and summed in bfloat16 or wider, within the bound.
No kernel may reach another device: no remote copies, remote signals or barrier semaphores. Data moves between devices by JAX's collectives and lax.ppermute only.
A program may use at most 64 MiB of HBM per device.

v0:
```python
import math
import jax
import jax.numpy as jnp
from jax import lax
from jax.sharding import PartitionSpec as P

NX = 128
REACH = 2


def extended(cells, sides, width):
    for axis, dim in sides:
        count = lax.axis_size(axis)
        ends = count - 1
        head = lax.slice_in_dim(cells, 0, width, axis=dim)
        tail = lax.slice_in_dim(cells, cells.shape[dim] - width, cells.shape[dim], axis=dim)
        cells = jnp.concatenate(
            [
                lax.ppermute(tail, axis, [(i, (i + 1) % count) for i in range(ends)]),
                cells,
                lax.ppermute(head, axis, [((i + 1) % count, i) for i in range(ends)]),
            ],
            axis=dim,
        )
    return cells


def make_tables(bins, freq_count):
    length = 2 * bins
    bin_index = lax.broadcasted_iota(jnp.int32, (freq_count, bins), 1)
    freq_index = lax.broadcasted_iota(jnp.int32, (freq_count, bins), 0)
    phase_angle = (bin_index * freq_index % length).astype(jnp.float32) * (2.0 * math.pi / length)
    kept_freq = freq_index >= 0
    weight = jnp.ones((freq_count, bins), jnp.float32)
    forward_table = jnp.concatenate(
        [
            jnp.where(kept_freq, jnp.cos(phase_angle), 0.0),
            jnp.where(kept_freq, -jnp.sin(phase_angle), 0.0),
        ],
        axis=0,
    ).astype(jnp.bfloat16)
    inverse_cos = (jnp.transpose(weight * jnp.cos(phase_angle)) / length).astype(jnp.bfloat16)
    inverse_sin = (jnp.transpose(-weight * jnp.sin(phase_angle)) / length).astype(jnp.bfloat16)
    return (forward_table, inverse_cos, inverse_sin)


def coagulate(gradients, amounts, coag_rate, tables, freq_count):
    forward_table, inverse_cos, inverse_sin = tables

    def one_level(pieces):
        gradient, particles, coefficient = pieces
        grad_spec = jnp.dot(forward_table, gradient, preferred_element_type=jnp.float32)
        mass_spec = jnp.dot(forward_table, particles, preferred_element_type=jnp.float32)
        grad_re = grad_spec[:freq_count]
        grad_im = grad_spec[freq_count:]
        mass_re = mass_spec[:freq_count]
        mass_im = mass_spec[freq_count:]
        prod_re = (mass_re * grad_re + mass_im * grad_im).astype(jnp.bfloat16)
        prod_im = (mass_re * grad_im - mass_im * grad_re).astype(jnp.bfloat16)
        correlation = jnp.dot(inverse_cos, prod_re, preferred_element_type=jnp.float32) + jnp.dot(
            inverse_sin, prod_im, preferred_element_type=jnp.float32
        )
        grad_wide = gradient.astype(jnp.float32)
        mass_wide = particles.astype(jnp.float32)
        total_mass = jnp.sum(mass_wide, axis=0)
        inner = jnp.sum(grad_wide * mass_wide, axis=0)
        return grad_wide + coefficient * (correlation - grad_wide * total_mass - inner)

    return lax.map(one_level, (gradients, amounts, coag_rate))


def body(cotangent, particles, coag_rate, courant, offsets, mass_flux, cloud_top):
    level_count, bins, cell_count = cotangent.shape
    row_count = cell_count // NX
    freq_count = 2 * bins
    tables = make_tables(bins, freq_count)
    adjoint = coagulate(cotangent, particles, coag_rate, tables, freq_count)
    adjoint = extended(adjoint.reshape(level_count, bins, row_count, NX), (("tile", 2),), REACH)
    centre_rows = adjoint[:, :, REACH : REACH + row_count, :]
    cour_y = courant[0].reshape(level_count, 1, row_count, NX)
    cour_x = courant[1].reshape(level_count, 1, row_count, NX)
    shift_y = offsets[0].reshape(row_count, NX)
    shift_x = offsets[1].reshape(row_count, NX)
    pad_x = jnp.pad(centre_rows, ((0, 0), (0, 0), (0, 0), (REACH, REACH)))
    along_y = jnp.zeros_like(centre_rows)
    along_x = jnp.zeros_like(centre_rows)
    for upwind in range(-REACH, REACH + 1):
        along_y = along_y + jnp.where(
            shift_y == upwind, adjoint[:, :, REACH + upwind : REACH + upwind + row_count, :], 0.0
        )
        along_x = along_x + jnp.where(
            shift_x == upwind, pad_x[:, :, :, REACH + upwind : REACH + upwind + NX], 0.0
        )
    remapped = centre_rows * (1.0 - cour_y - cour_x) + cour_y * along_y + cour_x * along_x
    remapped = remapped.astype(jnp.bfloat16).reshape(level_count, bins, cell_count)
    all_levels = mass_flux.shape[0]
    level_ids = lax.broadcasted_iota(jnp.int32, (all_levels, cloud_top.shape[0]), 0)
    inside = level_ids <= cloud_top[None, :]
    masked = jnp.where(
        inside[:, None, :] & inside[None, :, :], mass_flux, jnp.zeros_like(mass_flux)
    )
    received = lax.all_to_all(remapped, "lev", split_axis=2, concat_axis=0, tiled=True)
    mixing = jnp.einsum("obc,oic->ibc", received, masked, preferred_element_type=jnp.float32)
    return received.astype(jnp.float32) + mixing


def solution(mesh):
    placed = (
        P("lev", None, "tile"),
        P("lev", None, "tile"),
        P("lev"),
        P(None, "lev", "tile"),
        P(None, "tile"),
        P(None, None, ("tile", "lev")),
        P(("tile", "lev")),
    )
    return jax.shard_map(
        body, mesh=mesh, in_specs=placed, out_specs=P(None, None, ("tile", "lev")), check_vma=False
    )
```

profile of v0, /device:TPU:6, one launch (start us, length us, event | category | flops | bytes accessed | tf_op | source)
XLA Modules:
  0.0 171.8 jit_solution(14030658634548506464)
XLA Ops:
  0.5 72.2 %while.11 = (s32[]{:T(128)}, f32[9,96,1024]{2,1,0:T(8,128)}, bf16[9,96,1024]{2,1,0:T(8,128)(2,1)}, f32[9]{0:T(128)}, bf16[9,96,1024]{2,1,0:T(8,128)(2,1)}, /*index=5*/bf16[384,96]{1,0:T(8,128)(2,1)S(1)}, s32[]{:T(128)}) while((s32[]{:T(128)}, f32[9,96,1024]{2,1,0:T(8,128)}, bf16[9,96,1024]{2,1,0:T(8,128)(2,1)}, f32[9]{0:T(128)}, ...), condition=%wide.region_3.4_spmd.clone, body=%wide.region_0.3_spmd.clone.sunk | while | flops 229648384 | bytes 11766025 | solution.py:69
  0.5 1.3 convolution_bitcast_fusion.4
  1.8 1.3 convolution_bitcast_fusion.5
  3.7 1.1 convert_reduce_fusion.2
  4.8 0.7 dynamic_slice.35
  5.5 3.0 %fusion.83 = f32[9,96,1024]{2,1,0:T(8,128)} fusion(f32[9,96,1024]{2,1,0:T(8,128)} %get-tuple-element.142, s32[]{:T(128)} %get-tuple-element.141, f32[1024,96]{0,1:T(8,128)S(1)} %fusion.82, f32[384,1024]{1,0:T(8,128)S(1)} %convolution_bitcast_fusion.4, f32[384,1024]{1,0:T(8,128)S(1)} %convolution_bitcast_fusion.5, f32[1024]{0:T(1024)S(1)} %get-tuple-element.132, ...), kind=kOutput, calls=%fused_computation.11.clone.1 | convolution fusion | flops 39426048 | bytes 4137984 | tf_op jit(solution)/shard_map/while/body/eval_jaxpr/dot_general | solution.py:60
  8.5 1.3 convolution_bitcast_fusion.4
  9.8 1.3 convolution_bitcast_fusion.5
  11.7 1.1 convert_reduce_fusion.2
  12.8 0.7 dynamic_slice.35
  13.5 3.0 %fusion.83 = f32[9,96,1024]{2,1,0:T(8,128)} fusion(f32[9,96,1024]{2,1,0:T(8,128)} %get-tuple-element.142, s32[]{:T(128)} %get-tuple-element.141, f32[1024,96]{0,1:T(8,128)S(1)} %fusion.82, f32[384,1024]{1,0:T(8,128)S(1)} %convolution_bitcast_fusion.4, f32[384,1024]{1,0:T(8,128)S(1)} %convolution_bitcast_fusion.5, f32[1024]{0:T(1024)S(1)} %get-tuple-element.132, ...), kind=kOutput, calls=%fused_computation.11.clone.1 | convolution fusion | flops 39426048 | bytes 4137984 | tf_op jit(solution)/shard_map/while/body/eval_jaxpr/dot_general | solution.py:60
  16.5 1.3 convolution_bitcast_fusion.4
  17.8 1.3 convolution_bitcast_fusion.5
  19.7 1.1 convert_reduce_fusion.2
  20.9 0.7 dynamic_slice.35
  21.5 3.0 %fusion.83 = f32[9,96,1024]{2,1,0:T(8,128)} fusion(f32[9,96,1024]{2,1,0:T(8,128)} %get-tuple-element.142, s32[]{:T(128)} %get-tuple-element.141, f32[1024,96]{0,1:T(8,128)S(1)} %fusion.82, f32[384,1024]{1,0:T(8,128)S(1)} %convolution_bitcast_fusion.4, f32[384,1024]{1,0:T(8,128)S(1)} %convolution_bitcast_fusion.5, f32[1024]{0:T(1024)S(1)} %get-tuple-element.132, ...), kind=kOutput, calls=%fused_computation.11.clone.1 | convolution fusion | flops 39426048 | bytes 4137984 | tf_op jit(solution)/shard_map/while/body/eval_jaxpr/dot_general | solution.py:60
  24.6 1.3 convolution_bitcast_fusion.4
  25.9 1.3 convolution_bitcast_fusion.5
  27.8 1.1 convert_reduce_fusion.2
  29.6 3.0 %fusion.83 = f32[9,96,1024]{2,1,0:T(8,128)} fusion(f32[9,96,1024]{2,1,0:T(8,128)} %get-tuple-element.142, s32[]{:T(128)} %get-tuple-element.141, f32[1024,96]{0,1:T(8,128)S(1)} %fusion.82, f32[384,1024]{1,0:T(8,128)S(1)} %convolution_bitcast_fusion.4, f32[384,1024]{1,0:T(8,128)S(1)} %convolution_bitcast_fusion.5, f32[1024]{0:T(1024)S(1)} %get-tuple-element.132, ...), kind=kOutput, calls=%fused_computation.11.clone.1 | convolution fusion | flops 39426048 | bytes 4137984 | tf_op jit(solution)/shard_map/while/body/eval_jaxpr/dot_general | solution.py:60
  32.6 1.3 convolution_bitcast_fusion.4
  33.9 1.3 convolution_bitcast_fusion.5
  35.8 1.1 convert_reduce_fusion.2
  37.6 3.0 %fusion.83 = f32[9,96,1024]{2,1,0:T(8,128)} fusion(f32[9,96,1024]{2,1,0:T(8,128)} %get-tuple-element.142, s32[]{:T(128)} %get-tuple-element.141, f32[1024,96]{0,1:T(8,128)S(1)} %fusion.82, f32[384,1024]{1,0:T(8,128)S(1)} %convolution_bitcast_fusion.4, f32[384,1024]{1,0:T(8,128)S(1)} %convolution_bitcast_fusion.5, f32[1024]{0:T(1024)S(1)} %get-tuple-element.132, ...), kind=kOutput, calls=%fused_computation.11.clone.1 | convolution fusion | flops 39426048 | bytes 4137984 | tf_op jit(solution)/shard_map/while/body/eval_jaxpr/dot_general | solution.py:60
  40.6 1.3 convolution_bitcast_fusion.4
  41.9 1.3 convolution_bitcast_fusion.5
  43.8 1.1 convert_reduce_fusion.2
  44.9 0.7 dynamic_slice.35
  45.6 3.0 %fusion.83 = f32[9,96,1024]{2,1,0:T(8,128)} fusion(f32[9,96,1024]{2,1,0:T(8,128)} %get-tuple-element.142, s32[]{:T(128)} %get-tuple-element.141, f32[1024,96]{0,1:T(8,128)S(1)} %fusion.82, f32[384,1024]{1,0:T(8,128)S(1)} %convolution_bitcast_fusion.4, f32[384,1024]{1,0:T(8,128)S(1)} %convolution_bitcast_fusion.5, f32[1024]{0:T(1024)S(1)} %get-tuple-element.132, ...), kind=kOutput, calls=%fused_computation.11.clone.1 | convolution fusion | flops 39426048 | bytes 4137984 | tf_op jit(solution)/shard_map/while/body/eval_jaxpr/dot_general | solution.py:60
  48.6 1.3 convolution_bitcast_fusion.4
  49.9 1.3 convolution_bitcast_fusion.5
  51.8 1.1 convert_reduce_fusion.2
  53.0 0.7 dynamic_slice.35
  53.6 3.0 %fusion.83 = f32[9,96,1024]{2,1,0:T(8,128)} fusion(f32[9,96,1024]{2,1,0:T(8,128)} %get-tuple-element.142, s32[]{:T(128)} %get-tuple-element.141, f32[1024,96]{0,1:T(8,128)S(1)} %fusion.82, f32[384,1024]{1,0:T(8,128)S(1)} %convolution_bitcast_fusion.4, f32[384,1024]{1,0:T(8,128)S(1)} %convolution_bitcast_fusion.5, f32[1024]{0:T(1024)S(1)} %get-tuple-element.132, ...), kind=kOutput, calls=%fused_computation.11.clone.1 | convolution fusion | flops 39426048 | bytes 4137984 | tf_op jit(solution)/shard_map/while/body/eval_jaxpr/dot_general | solution.py:60
  56.7 1.3 convolution_bitcast_fusion.4
  58.0 1.3 convolution_bitcast_fusion.5
  59.9 1.1 convert_reduce_fusion.2
  61.0 0.7 dynamic_slice.35
  61.7 3.0 %fusion.83 = f32[9,96,1024]{2,1,0:T(8,128)} fusion(f32[9,96,1024]{2,1,0:T(8,128)} %get-tuple-element.142, s32[]{:T(128)} %get-tuple-element.141, f32[1024,96]{0,1:T(8,128)S(1)} %fusion.82, f32[384,1024]{1,0:T(8,128)S(1)} %convolution_bitcast_fusion.4, f32[384,1024]{1,0:T(8,128)S(1)} %convolution_bitcast_fusion.5, f32[1024]{0:T(1024)S(1)} %get-tuple-element.132, ...), kind=kOutput, calls=%fused_computation.11.clone.1 | convolution fusion | flops 39426048 | bytes 4137984 | tf_op jit(solution)/shard_map/while/body/eval_jaxpr/dot_general | solution.py:60
  64.7 1.3 convolution_bitcast_fusion.4
  66.0 1.3 convolution_bitcast_fusion.5
  67.9 1.1 convert_reduce_fusion.2
  69.7 3.0 %fusion.83 = f32[9,96,1024]{2,1,0:T(8,128)} fusion(f32[9,96,1024]{2,1,0:T(8,128)} %get-tuple-element.142, s32[]{:T(128)} %get-tuple-element.141, f32[1024,96]{0,1:T(8,128)S(1)} %fusion.82, f32[384,1024]{1,0:T(8,128)S(1)} %convolution_bitcast_fusion.4, f32[384,1024]{1,0:T(8,128)S(1)} %convolution_bitcast_fusion.5, f32[1024]{0:T(1024)S(1)} %get-tuple-element.132, ...), kind=kOutput, calls=%fused_computation.11.clone.1 | convolution fusion | flops 39426048 | bytes 4137984 | tf_op jit(solution)/shard_map/while/body/eval_jaxpr/dot_general | solution.py:60
  72.7 2.8 %copy.77 = f32[108,8,8,128]{3,2,1,0:T(8,128)S(1)} copy(f32[108,8,8,128]{3,1,2,0:T(8,128)} %bitcast.27) | data formatting | bytes 7077888
  75.6 0.7 fusion.65
  76.3 1.9 %collective-permute-start = (f32[9,96,2,128]{3,1,2,0:T(8,128)S(1)}, f32[9,96,2,128]{3,1,2,0:T(8,128)S(1)}, u32[]{:S(2)}, u32[]{:S(2)}) collective-permute-start(f32[9,96,2,128]{3,1,2,0:T(8,128)S(1)} %copy.64), channel_id=1, source_target_pairs={{0,1},{1,2},{2,3},{3,4},{4,5},{5,6},{6,7},{7,8},{8,9},{9,10},{10,1... | collective-permute-start | bytes 2654216 | tf_op jit(solution)/shard_map/ppermute | solution.py:19
  78.4 8.1 %collective-permute-start.1 = (f32[9,96,2,128]{3,1,2,0:T(8,128)S(1)}, f32[9,96,2,128]{3,1,2,0:T(8,128)S(1)}, u32[]{:S(2)}, u32[]{:S(2)}) collective-permute-start(f32[9,96,2,128]{3,1,2,0:T(8,128)S(1)} %copy.66), channel_id=1, source_target_pairs={{1,0},{2,1},{3,2},{4,3},{5,4},{6,5},{7,6},{8,7},{9,8},{10,9},{11,1... | collective-permute-start | bytes 2654216 | tf_op jit(solution)/shard_map/ppermute | solution.py:21
  87.5 7.6 %collective-permute-done = f32[9,96,2,128]{3,1,2,0:T(8,128)S(1)} collective-permute-done((f32[9,96,2,128]{3,1,2,0:T(8,128)S(1)}, f32[9,96,2,128]{3,1,2,0:T(8,128)S(1)}, u32[]{:S(2)}, u32[]{:S(2)}) %collective-permute-start) | collective-permute-done | bytes 884768 | tf_op jit(solution)/shard_map/ppermute | solution.py:19
  95.1 0.7 copy.65
  95.8 1.2 collective-permute-done.1
  97.0 1.0 copy_dynamic-update-slice_fusion
  98.0 6.1 %fusion.49 = bf16[9,96,8,128]{3,2,1,0:T(8,128)(2,1)S(1)} fusion(f32[9,96,2,128]{3,2,1,0:T(2,128)S(1)} %copy.65, f32[9,96,8,128]{3,2,1,0:T(8,128)S(1)} %bitcast.90, f32[9,96,10,128]{3,2,1,0:T(8,128)S(1)} %copy_dynamic-update-slice_fusion, f32[9,8,128]{2,1,0:T(8,128)S(1)} %bitcast.97, f32[9,8,128]{2,1,0:T(8,128)S(1)} %bitcast.95, ...), kind=kLoop, calls=%fused_computation.63 | loop fusion | flops 23003136 | bytes 13391872 | tf_op jit(solution)/shard_map/convert_element_type | solution.py:95
  104.1 4.7 %copy.74 = bf16[9,96,8,128]{1,0,3,2:T(8,128)(2,1)} copy(bf16[9,96,8,128]{3,2,1,0:T(8,128)(2,1)S(1)} %fusion.49) | data formatting | bytes 3538944 | tf_op jit(solution)/shard_map/reshape | solution.py:95
  108.8 8.0 %reshape.88 = bf16[8,2,55296]{2,1,0:T(2,128)(2,1)} reshape(bf16[1024,9,96]{2,1,0:T(8,128)(2,1)} %bitcast.91) | data formatting | bytes 3538944
  116.8 5.9 %all-to-all-start = ((bf16[8,2,55296]{2,1,0:T(2,128)(2,1)}), bf16[8,2,55296]{2,1,0:T(2,128)(2,1)S(1)}, u32[]{:S(2)}, u32[]{:S(2)}) async-start(bf16[8,2,55296]{2,1,0:T(2,128)(2,1)} %reshape.88), calls=%async_computation | async-start | bytes 3538944 | tf_op jit(solution)/shard_map/all_to_all | solution.py:102
  122.7 1.8 %and_select_fusion = bf16[72,72,128]{2,1,0:T(8,128)(2,1)S(1)} fusion(bf16[72,72,128]{2,1,0:T(8,128)(2,1)} %param.14, pred[72,128]{1,0:T(8,128)(4,1)S(1)} %iota_compare_fusion), kind=kLoop, calls=%fused_computation.78 | loop fusion | flops 1327104 | bytes 2663424 | tf_op jit(solution)/shard_map/jit(_where)/select_n | solution.py:99
  124.5 2.7 %copy.71 = bf16[72,72,128]{0,1,2:T(8,128)(2,1)} copy(bf16[72,72,128]{2,1,0:T(8,128)(2,1)S(1)} %and_select_fusion) | data formatting | bytes 2654208 | tf_op jit(solution)/shard_map/jit(_where)/select_n | solution.py:99
  127.3 15.6 %all-to-all-done = bf16[8,2,55296]{2,1,0:T(2,128)(2,1)S(1)} async-done(((bf16[8,2,55296]{2,1,0:T(2,128)(2,1)}), bf16[8,2,55296]{2,1,0:T(2,128)(2,1)S(1)}, u32[]{:S(2)}, u32[]{:S(2)}) %all-to-all-start) | async-done | bytes 1769504 | tf_op jit(solution)/shard_map/all_to_all | solution.py:102
  142.9 6.2 %reshape.89 = bf16[1024,9,96]{2,1,0:T(8,128)(2,1)} reshape(bf16[8,2,55296]{2,1,0:T(2,128)(2,1)S(1)} %all-to-all-done) | data formatting | bytes 3538944
  149.1 4.1 %copy.70 = bf16[8,9,96,128]{3,2,1,0:T(8,128)(2,1)S(1)} copy(bf16[8,9,96,128]{2,1,3,0:T(8,128)(2,1)} %bitcast.92) | data formatting | bytes 3538944 | tf_op jit(solution)/shard_map/all_to_all | solution.py:102
  153.2 2.7 %copy.72 = bf16[72,96,128]{1,0,2:T(8,128)(2,1)} copy(bf16[72,96,128]{2,1,0:T(8,128)(2,1)S(1)} %bitcast.93) | data formatting | bytes 3538944 | tf_op jit(solution)/shard_map/all_to_all | solution.py:102
  156.0 5.9 %fusion.67 = f32[128,72,96]{2,1,0:T(8,128)} fusion(bf16[72,72,128]{0,1,2:T(8,128)(2,1)} %copy.71, bf16[72,96,128]{1,0,2:T(8,128)(2,1)} %copy.72), kind=kOutput, calls=%fused_computation.105 | convolution fusion | flops 127401984 | bytes 6635520 | tf_op jit(solution)/shard_map/obc,oic->ibc/dot_general | solution.py:103
  161.9 5.7 %copy.73 = f32[128,72,96]{0,2,1:T(8,128)} copy(f32[128,72,96]{2,1,0:T(8,128)} %fusion.67) | data formatting | bytes 7077888 | tf_op jit(solution)/shard_map/obc,oic->ibc/dot_general | solution.py:103
  167.5 4.3 %bitcast_add_fusion = f32[72,96,128]{2,1,0:T(8,128)} fusion(f32[128,72,96]{0,2,1:T(8,128)} %copy.73, bf16[8,9,96,128]{3,2,1,0:T(8,128)(2,1)S(1)} %copy.70), kind=kLoop, calls=%fused_computation.77 | loop fusion | flops 1769472 | bytes 8847360 | tf_op jit(solution)/shard_map/add | solution.py:104
  (46 shorter events, 9.4 us)
Async XLA Ops:
  0.5 4.3 %copy-start.3 = (f32[9]{0:T(128)S(1)}, f32[9]{0:T(128)}, u32[]{:S(2)}) copy-start(f32[9]{0:T(128)} %get-tuple-element.151) | copy-start | bytes 112 | tf_op jit(solution)/shard_map/while
  8.5 4.3 %copy-start.3 = (f32[9]{0:T(128)S(1)}, f32[9]{0:T(128)}, u32[]{:S(2)}) copy-start(f32[9]{0:T(128)} %get-tuple-element.151) | copy-start | bytes 112 | tf_op jit(solution)/shard_map/while
  16.5 4.3 %copy-start.3 = (f32[9]{0:T(128)S(1)}, f32[9]{0:T(128)}, u32[]{:S(2)}) copy-start(f32[9]{0:T(128)} %get-tuple-element.151) | copy-start | bytes 112 | tf_op jit(solution)/shard_map/while
  24.6 4.3 %copy-start.3 = (f32[9]{0:T(128)S(1)}, f32[9]{0:T(128)}, u32[]{:S(2)}) copy-start(f32[9]{0:T(128)} %get-tuple-element.151) | copy-start | bytes 112 | tf_op jit(solution)/shard_map/while
  32.6 4.3 %copy-start.3 = (f32[9]{0:T(128)S(1)}, f32[9]{0:T(128)}, u32[]{:S(2)}) copy-start(f32[9]{0:T(128)} %get-tuple-element.151) | copy-start | bytes 112 | tf_op jit(solution)/shard_map/while
  40.6 4.3 %copy-start.3 = (f32[9]{0:T(128)S(1)}, f32[9]{0:T(128)}, u32[]{:S(2)}) copy-start(f32[9]{0:T(128)} %get-tuple-element.151) | copy-start | bytes 112 | tf_op jit(solution)/shard_map/while
  48.6 4.3 %copy-start.3 = (f32[9]{0:T(128)S(1)}, f32[9]{0:T(128)}, u32[]{:S(2)}) copy-start(f32[9]{0:T(128)} %get-tuple-element.151) | copy-start | bytes 112 | tf_op jit(solution)/shard_map/while
  56.7 4.3 %copy-start.3 = (f32[9]{0:T(128)S(1)}, f32[9]{0:T(128)}, u32[]{:S(2)}) copy-start(f32[9]{0:T(128)} %get-tuple-element.151) | copy-start | bytes 112 | tf_op jit(solution)/shard_map/while
  64.7 4.3 %copy-start.3 = (f32[9]{0:T(128)S(1)}, f32[9]{0:T(128)}, u32[]{:S(2)}) copy-start(f32[9]{0:T(128)} %get-tuple-element.151) | copy-start | bytes 112 | tf_op jit(solution)/shard_map/while
  75.6 10.9 %copy-start.1 = (s32[2,1024]{1,0:T(2,128)S(1)}, s32[2,1024]{1,0:T(2,128)}, u32[]{:S(2)}) copy-start(s32[2,1024]{1,0:T(2,128)} %param.13) | copy-start | bytes 24580
  76.3 18.8 %collective-permute-start = (f32[9,96,2,128]{3,1,2,0:T(8,128)S(1)}, f32[9,96,2,128]{3,1,2,0:T(8,128)S(1)}, u32[]{:S(2)}, u32[]{:S(2)}) collective-permute-start(f32[9,96,2,128]{3,1,2,0:T(8,128)S(1)} %copy.64), channel_id=1, source_target_pairs={{0,1},{1,2},{2,3},{3,4},{4,5},{5,6},{6,7},{7,8},{8,9},{9,10},{10,1... | collective-permute-start | bytes 2654216 | tf_op jit(solution)/shard_map/ppermute | solution.py:19
  78.4 18.6 %collective-permute-start.1 = (f32[9,96,2,128]{3,1,2,0:T(8,128)S(1)}, f32[9,96,2,128]{3,1,2,0:T(8,128)S(1)}, u32[]{:S(2)}, u32[]{:S(2)}) collective-permute-start(f32[9,96,2,128]{3,1,2,0:T(8,128)S(1)} %copy.66), channel_id=1, source_target_pairs={{1,0},{2,1},{3,2},{4,3},{5,4},{6,5},{7,6},{8,7},{9,8},{10,9},{11,1... | collective-permute-start | bytes 2654216 | tf_op jit(solution)/shard_map/ppermute | solution.py:21
  86.6 0.9 copy-start
  108.8 14.0 %copy-start.2 = (s32[128]{0:T(128)S(1)}, s32[128]{0:T(128)}, u32[]{:S(2)}) copy-start(s32[128]{0:T(128)} %param.15) | copy-start | bytes 1540
  116.8 26.1 %all-to-all-start = ((bf16[8,2,55296]{2,1,0:T(2,128)(2,1)}), bf16[8,2,55296]{2,1,0:T(2,128)(2,1)S(1)}, u32[]{:S(2)}, u32[]{:S(2)}) async-start(bf16[8,2,55296]{2,1,0:T(2,128)(2,1)} %reshape.88), calls=%async_computation | async-start | bytes 3538944 | tf_op jit(solution)/shard_map/all_to_all | solution.py:102
where the time goes:
time: 173 us; the launch traced here: 172 us
  matrix products  61.8 us (36%)
  local copies, waits for them, and re-layouts  46.5 us (27%)
  waiting for transfers between devices  24.4 us (14%)
  other arithmetic  22.9 us (13%)
  starting transfers between devices  15.9 us (9%)
    dot_general x9, matrix products, one_level(): jnp.dot(inverse_sin, prod_im, preferred_element_type=jnp.float32)  27.2 us
    unnamed x10, local copies, waits for them, and re-layouts  17.9 us
    all_to_all x1, waiting for transfers between devices, body(): lax.all_to_all(remapped, 'lev', split_axis=2, concat_axis=0, tiled=True)  15.6 us
    dot_general x9, matrix products, one_level(): jnp.dot(forward_table, gradient, preferred_element_type=jnp.float32)  11.6 us
    dot_general x9, matrix products, one_level(): jnp.dot(forward_table, particles, preferred_element_type=jnp.float32)  11.5 us
    reduce_sum x9, other arithmetic, one_level(): total_mass = jnp.sum(mass_wide, axis=0)  10 us
    ppermute x1, starting transfers between devices, extended(): lax.ppermute(head, axis, [((i + 1) % count, i) for i in range(ends)])  8.05 us
    ppermute x1, waiting for transfers between devices, extended(): lax.ppermute(tail, axis, [(i, (i + 1) % count) for i in range(ends)])  7.59 us
  transfers between devices with their start and end apart: 3, of which 3 were waited for; matrix products, arithmetic and copies ran while one was open for 3% of the time, Pallas kernels for 0%

commit v1 on v0

--- a/solution.py
+++ b/solution.py
@@ -99,7 +99,10 @@
     masked = jnp.where(
         inside[:, None, :] & inside[None, :, :], mass_flux, jnp.zeros_like(mass_flux)
     )
-    received = lax.all_to_all(remapped, "lev", split_axis=2, concat_axis=0, tiled=True)
+    received = jnp.concatenate(
+        lax.all_to_all(jnp.stack(jnp.split(remapped, lax.axis_size("lev"), axis=2)), "lev", 0, 0),
+        axis=0,
+    )
     mixing = jnp.einsum("obc,oic->ibc", received, masked, preferred_element_type=jnp.float32)
     return received.astype(jnp.float32) + mixing
 

time: 173 us -> 155 us (0.90)
  local copies, waits for them, and re-layouts: 46.5 us -> 28.8 us
    unnamed x10 -> x15, local copies, waits for them, and re-layouts: 17.9 us -> 8.91 us
    all_to_all x2 -> x0, local copies, waits for them, and re-layouts: 6.87 us -> none  [body(): lax.all_to_all(remapped, 'lev', split_axis=2, concat_axis=0, tiled=True)]
    ppermute x1, waiting for transfers between devices: 1.16 us -> 7.51 us  [extended(): lax.ppermute(head, axis, [((i + 1) % count, i) for i in range(ends)])]
    all_to_all x1, waiting for transfers between devices: 15.6 us -> 9.34 us  [body(): lax.all_to_all(jnp.stack(jnp.split(remapped, lax.axis_size('lev'), axis=2...]
    reshape x1, local copies, waits for them, and re-layouts: 4.68 us -> 0.81 us  [body(): remapped.astype(jnp.bfloat16).reshape(level_count, bins, cell_count)]
    reshape x0 -> x1, local copies, waits for them, and re-layouts: none -> 2.74 us  [body(): jnp.concatenate(lax.all_to_all(jnp.stack(jnp.split(remapped, lax.axis_siz...]
  transfers between devices with their start and end apart: 3 -> 3, of which waited for: 3 -> 3; matrix products, arithmetic and copies ran while one was open for 3% -> 4% of each run, Pallas kernels for 0% -> 0%
where the time goes in v1:
time: 155 us; the launch traced here: 154 us
  matrix products  61.6 us (40%)
  local copies, waits for them, and re-layouts  28.8 us (19%)
  waiting for transfers between devices  23.9 us (15%)
  other arithmetic  22.8 us (15%)
  starting transfers between devices  15.9 us (10%)
    dot_general x9, matrix products, one_level(): jnp.dot(inverse_sin, prod_im, preferred_element_type=jnp.float32)  27.2 us
    dot_general x9, matrix products, one_level(): jnp.dot(forward_table, particles, preferred_element_type=jnp.float32)  11.5 us
    dot_general x9, matrix products, one_level(): jnp.dot(forward_table, gradient, preferred_element_type=jnp.float32)  11.4 us
    reduce_sum x9, other arithmetic, one_level(): total_mass = jnp.sum(mass_wide, axis=0)  10 us
    all_to_all x1, waiting for transfers between devices, body(): lax.all_to_all(jnp.stack(jnp.split(remapped, lax.axis_size('lev'), axis=2...  9.34 us
    unnamed x15, local copies, waits for them, and re-layouts  8.91 us
    ppermute x1, starting transfers between devices, extended(): lax.ppermute(head, axis, [((i + 1) % count, i) for i in range(ends)])  8.05 us
    ppermute x1, waiting for transfers between devices, extended(): lax.ppermute(head, axis, [((i + 1) % count, i) for i in range(ends)])  7.51 us
  transfers between devices with their start and end apart: 3, of which 3 were waited for; matrix products, arithmetic and copies ran while one was open for 4% of the time, Pallas kernels for 0%

profile of v1, /device:TPU:6, one launch (start us, length us, event | category | flops | bytes accessed | tf_op | source)
XLA Modules:
  0.0 153.5 jit_solution(11630961382888933139)
XLA Ops:
  0.5 72.2 %while.11 = (s32[]{:T(128)}, f32[9,96,1024]{2,1,0:T(8,128)}, bf16[9,96,1024]{2,1,0:T(8,128)(2,1)}, f32[9]{0:T(128)}, bf16[9,96,1024]{2,1,0:T(8,128)(2,1)}, /*index=5*/bf16[384,96]{1,0:T(8,128)(2,1)S(1)}, s32[]{:T(128)}) while((s32[]{:T(128)}, f32[9,96,1024]{2,1,0:T(8,128)}, bf16[9,96,1024]{2,1,0:T(8,128)(2,1)}, f32[9]{0:T(128)}, ...), condition=%wide.region_3.4_spmd.clone, body=%wide.region_0.3_spmd.clone.sunk | while | flops 229648384 | bytes 11766025 | solution.py:69
  0.5 1.3 convolution_bitcast_fusion.4
  1.8 1.3 convolution_bitcast_fusion.5
  3.7 1.1 convert_reduce_fusion.2
  4.8 0.7 dynamic_slice.35
  5.5 3.0 %fusion.91 = f32[9,96,1024]{2,1,0:T(8,128)} fusion(f32[9,96,1024]{2,1,0:T(8,128)} %get-tuple-element.142, s32[]{:T(128)} %get-tuple-element.141, f32[1024,96]{0,1:T(8,128)S(1)} %fusion.90, f32[384,1024]{1,0:T(8,128)S(1)} %convolution_bitcast_fusion.4, f32[384,1024]{1,0:T(8,128)S(1)} %convolution_bitcast_fusion.5, f32[1024]{0:T(1024)S(1)} %get-tuple-element.132, ...), kind=kOutput, calls=%fused_computation.11.clone.1 | convolution fusion | flops 39426048 | bytes 4137984 | tf_op jit(solution)/shard_map/while/body/eval_jaxpr/dot_general | solution.py:60
  8.5 1.3 convolution_bitcast_fusion.4
  9.8 1.3 convolution_bitcast_fusion.5
  11.7 1.1 convert_reduce_fusion.2
  13.5 3.0 %fusion.91 = f32[9,96,1024]{2,1,0:T(8,128)} fusion(f32[9,96,1024]{2,1,0:T(8,128)} %get-tuple-element.142, s32[]{:T(128)} %get-tuple-element.141, f32[1024,96]{0,1:T(8,128)S(1)} %fusion.90, f32[384,1024]{1,0:T(8,128)S(1)} %convolution_bitcast_fusion.4, f32[384,1024]{1,0:T(8,128)S(1)} %convolution_bitcast_fusion.5, f32[1024]{0:T(1024)S(1)} %get-tuple-element.132, ...), kind=kOutput, calls=%fused_computation.11.clone.1 | convolution fusion | flops 39426048 | bytes 4137984 | tf_op jit(solution)/shard_map/while/body/eval_jaxpr/dot_general | solution.py:60
  16.5 1.3 convolution_bitcast_fusion.4
  17.8 1.3 convolution_bitcast_fusion.5
  19.7 1.1 convert_reduce_fusion.2
  21.5 3.0 %fusion.91 = f32[9,96,1024]{2,1,0:T(8,128)} fusion(f32[9,96,1024]{2,1,0:T(8,128)} %get-tuple-element.142, s32[]{:T(128)} %get-tuple-element.141, f32[1024,96]{0,1:T(8,128)S(1)} %fusion.90, f32[384,1024]{1,0:T(8,128)S(1)} %convolution_bitcast_fusion.4, f32[384,1024]{1,0:T(8,128)S(1)} %convolution_bitcast_fusion.5, f32[1024]{0:T(1024)S(1)} %get-tuple-element.132, ...), kind=kOutput, calls=%fused_computation.11.clone.1 | convolution fusion | flops 39426048 | bytes 4137984 | tf_op jit(solution)/shard_map/while/body/eval_jaxpr/dot_general | solution.py:60
  24.5 1.3 convolution_bitcast_fusion.4
  25.8 1.3 convolution_bitcast_fusion.5
  27.8 1.1 convert_reduce_fusion.2
  28.9 0.7 dynamic_slice.35
  29.5 3.0 %fusion.91 = f32[9,96,1024]{2,1,0:T(8,128)} fusion(f32[9,96,1024]{2,1,0:T(8,128)} %get-tuple-element.142, s32[]{:T(128)} %get-tuple-element.141, f32[1024,96]{0,1:T(8,128)S(1)} %fusion.90, f32[384,1024]{1,0:T(8,128)S(1)} %convolution_bitcast_fusion.4, f32[384,1024]{1,0:T(8,128)S(1)} %convolution_bitcast_fusion.5, f32[1024]{0:T(1024)S(1)} %get-tuple-element.132, ...), kind=kOutput, calls=%fused_computation.11.clone.1 | convolution fusion | flops 39426048 | bytes 4137984 | tf_op jit(solution)/shard_map/while/body/eval_jaxpr/dot_general | solution.py:60
  32.6 1.3 convolution_bitcast_fusion.4
  33.9 1.3 convolution_bitcast_fusion.5
  35.8 1.1 convert_reduce_fusion.2
  36.9 0.7 dynamic_slice.35
  37.6 3.0 %fusion.91 = f32[9,96,1024]{2,1,0:T(8,128)} fusion(f32[9,96,1024]{2,1,0:T(8,128)} %get-tuple-element.142, s32[]{:T(128)} %get-tuple-element.141, f32[1024,96]{0,1:T(8,128)S(1)} %fusion.90, f32[384,1024]{1,0:T(8,128)S(1)} %convolution_bitcast_fusion.4, f32[384,1024]{1,0:T(8,128)S(1)} %convolution_bitcast_fusion.5, f32[1024]{0:T(1024)S(1)} %get-tuple-element.132, ...), kind=kOutput, calls=%fused_computation.11.clone.1 | convolution fusion | flops 39426048 | bytes 4137984 | tf_op jit(solution)/shard_map/while/body/eval_jaxpr/dot_general | solution.py:60
  40.6 1.3 convolution_bitcast_fusion.4
  41.9 1.3 convolution_bitcast_fusion.5
  43.8 1.1 convert_reduce_fusion.2
  45.6 3.0 %fusion.91 = f32[9,96,1024]{2,1,0:T(8,128)} fusion(f32[9,96,1024]{2,1,0:T(8,128)} %get-tuple-element.142, s32[]{:T(128)} %get-tuple-element.141, f32[1024,96]{0,1:T(8,128)S(1)} %fusion.90, f32[384,1024]{1,0:T(8,128)S(1)} %convolution_bitcast_fusion.4, f32[384,1024]{1,0:T(8,128)S(1)} %convolution_bitcast_fusion.5, f32[1024]{0:T(1024)S(1)} %get-tuple-element.132, ...), kind=kOutput, calls=%fused_computation.11.clone.1 | convolution fusion | flops 39426048 | bytes 4137984 | tf_op jit(solution)/shard_map/while/body/eval_jaxpr/dot_general | solution.py:60
  48.6 1.3 convolution_bitcast_fusion.4
  49.9 1.3 convolution_bitcast_fusion.5
  51.8 1.1 convert_reduce_fusion.2
  53.6 3.0 %fusion.91 = f32[9,96,1024]{2,1,0:T(8,128)} fusion(f32[9,96,1024]{2,1,0:T(8,128)} %get-tuple-element.142, s32[]{:T(128)} %get-tuple-element.141, f32[1024,96]{0,1:T(8,128)S(1)} %fusion.90, f32[384,1024]{1,0:T(8,128)S(1)} %convolution_bitcast_fusion.4, f32[384,1024]{1,0:T(8,128)S(1)} %convolution_bitcast_fusion.5, f32[1024]{0:T(1024)S(1)} %get-tuple-element.132, ...), kind=kOutput, calls=%fused_computation.11.clone.1 | convolution fusion | flops 39426048 | bytes 4137984 | tf_op jit(solution)/shard_map/while/body/eval_jaxpr/dot_general | solution.py:60
  56.6 1.3 convolution_bitcast_fusion.4
  57.9 1.3 convolution_bitcast_fusion.5
  59.8 1.1 convert_reduce_fusion.2
  61.6 3.0 %fusion.91 = f32[9,96,1024]{2,1,0:T(8,128)} fusion(f32[9,96,1024]{2,1,0:T(8,128)} %get-tuple-element.142, s32[]{:T(128)} %get-tuple-element.141, f32[1024,96]{0,1:T(8,128)S(1)} %fusion.90, f32[384,1024]{1,0:T(8,128)S(1)} %convolution_bitcast_fusion.4, f32[384,1024]{1,0:T(8,128)S(1)} %convolution_bitcast_fusion.5, f32[1024]{0:T(1024)S(1)} %get-tuple-element.132, ...), kind=kOutput, calls=%fused_computation.11.clone.1 | convolution fusion | flops 39426048 | bytes 4137984 | tf_op jit(solution)/shard_map/while/body/eval_jaxpr/dot_general | solution.py:60
  64.7 1.3 convolution_bitcast_fusion.4
  65.9 1.3 convolution_bitcast_fusion.5
  67.9 1.1 convert_reduce_fusion.2
  69.7 3.0 %fusion.91 = f32[9,96,1024]{2,1,0:T(8,128)} fusion(f32[9,96,1024]{2,1,0:T(8,128)} %get-tuple-element.142, s32[]{:T(128)} %get-tuple-element.141, f32[1024,96]{0,1:T(8,128)S(1)} %fusion.90, f32[384,1024]{1,0:T(8,128)S(1)} %convolution_bitcast_fusion.4, f32[384,1024]{1,0:T(8,128)S(1)} %convolution_bitcast_fusion.5, f32[1024]{0:T(1024)S(1)} %get-tuple-element.132, ...), kind=kOutput, calls=%fused_computation.11.clone.1 | convolution fusion | flops 39426048 | bytes 4137984 | tf_op jit(solution)/shard_map/while/body/eval_jaxpr/dot_general | solution.py:60
  72.7 2.8 %copy.25 = f32[108,8,8,128]{3,2,1,0:T(8,128)S(1)} copy(f32[108,8,8,128]{3,1,2,0:T(8,128)} %bitcast.30) | data formatting | bytes 7077888
  75.5 0.7 fusion.73
  76.2 8.0 %collective-permute-start.1 = (f32[9,96,2,128]{3,2,1,0:T(2,128)S(1)}, f32[9,96,2,128]{3,2,1,0:T(2,128)S(1)}, u32[]{:S(2)}, u32[]{:S(2)}) collective-permute-start(f32[9,96,2,128]{3,2,1,0:T(2,128)S(1)} %get-tuple-element.87), channel_id=1, source_target_pairs={{1,0},{2,1},{3,2},{4,3},{5,4},{6,5},{7,6},{8,7},{9,8},{10,9},{11,1... | collective-permute-start | bytes 2654216 | tf_op jit(solution)/shard_map/ppermute | solution.py:21
  84.3 1.9 %collective-permute-start = (f32[9,96,2,128]{3,2,1,0:T(2,128)S(1)}, f32[9,96,2,128]{3,2,1,0:T(2,128)S(1)}, u32[]{:S(2)}, u32[]{:S(2)}) collective-permute-start(f32[9,96,2,128]{3,2,1,0:T(2,128)S(1)} %get-tuple-element.88), channel_id=1, source_target_pairs={{0,1},{1,2},{2,3},{3,4},{4,5},{5,6},{6,7},{7,8},{8,9},{9,10},{10,1... | collective-permute-start | bytes 2654216 | tf_op jit(solution)/shard_map/ppermute | solution.py:19
  87.3 7.5 %collective-permute-done.1 = f32[9,96,2,128]{3,2,1,0:T(2,128)S(1)} collective-permute-done((f32[9,96,2,128]{3,2,1,0:T(2,128)S(1)}, f32[9,96,2,128]{3,2,1,0:T(2,128)S(1)}, u32[]{:S(2)}, u32[]{:S(2)}) %collective-permute-start.1) | collective-permute-done | bytes 884768 | tf_op jit(solution)/shard_map/ppermute | solution.py:21
  95.2 7.1 %collective-permute-done = f32[9,96,2,128]{3,2,1,0:T(2,128)S(1)} collective-permute-done((f32[9,96,2,128]{3,2,1,0:T(2,128)S(1)}, f32[9,96,2,128]{3,2,1,0:T(2,128)S(1)}, u32[]{:S(2)}, u32[]{:S(2)}) %collective-permute-start) | collective-permute-done | bytes 884768 | tf_op jit(solution)/shard_map/ppermute | solution.py:19
  102.2 6.1 %fusion.49 = bf16[9,96,8,128]{3,2,1,0:T(8,128)(2,1)S(1)} fusion(f32[9,96,2,128]{3,2,1,0:T(2,128)S(1)} %collective-permute-done, f32[9,96,8,128]{3,2,1,0:T(8,128)S(1)} %bitcast.117, f32[9,96,10,128]{3,2,1,0:T(8,128)S(1)} %constant_dynamic-update-slice_fusion, f32[9,8,128]{2,1,0:T(8,128)S(1)} %bitcast.122, f32[9,8,128]{2,1,0:T(8,128)S(1)} %bitcast.120, ...), kind=kLoop, calls=%fused_computation.63 | loop fusion | flops 23003136 | bytes 13391872 | tf_op jit(solution)/shard_map/convert_element_type | solution.py:95
  108.4 0.8 reshape.80
  109.2 0.7 fusion.67
  109.9 0.8 fusion.66
  110.7 0.7 fusion.65
  111.4 0.7 fusion.64
  112.1 0.7 fusion.63
  112.9 0.7 fusion.62
  113.6 0.8 fusion.61
  114.4 0.7 fusion.60
  115.1 5.9 %all-to-all-start = ((bf16[8,9,96,128]{3,2,1,0:T(8,128)(2,1)}), bf16[8,9,96,128]{3,2,1,0:T(8,128)(2,1)S(1)}, u32[]{:S(2)}, u32[]{:S(2)}) async-start(bf16[8,9,96,128]{3,2,1,0:T(8,128)(2,1)} %fusion.60), calls=%async_computation | async-start | bytes 3538944 | tf_op jit(solution)/shard_map/all_to_all | solution.py:103
  121.1 1.8 %and_select_fusion = bf16[72,72,128]{2,1,0:T(8,128)(2,1)S(1)} fusion(bf16[72,72,128]{2,1,0:T(8,128)(2,1)} %param.14, pred[72,128]{1,0:T(8,128)(4,1)S(1)} %iota_compare_fusion), kind=kLoop, calls=%fused_computation.78 | loop fusion | flops 1327104 | bytes 2663424 | tf_op jit(solution)/shard_map/jit(_where)/select_n | solution.py:99
  122.9 2.7 %copy.22 = bf16[72,72,128]{0,1,2:T(8,128)(2,1)} copy(bf16[72,72,128]{2,1,0:T(8,128)(2,1)S(1)} %and_select_fusion) | data formatting | bytes 2654208 | tf_op jit(solution)/shard_map/jit(_where)/select_n | solution.py:99
  125.6 9.3 %all-to-all-done = bf16[8,9,96,128]{3,2,1,0:T(8,128)(2,1)S(1)} async-done(((bf16[8,9,96,128]{3,2,1,0:T(8,128)(2,1)}), bf16[8,9,96,128]{3,2,1,0:T(8,128)(2,1)S(1)}, u32[]{:S(2)}, u32[]{:S(2)}) %all-to-all-start) | async-done | bytes 1769504 | tf_op jit(solution)/shard_map/all_to_all | solution.py:103
  134.9 2.7 %copy.23 = bf16[72,96,128]{1,0,2:T(8,128)(2,1)} copy(bf16[72,96,128]{2,1,0:T(8,128)(2,1)S(1)} %bitcast.118) | data formatting | bytes 3538944 | tf_op jit(solution)/shard_map/reshape | solution.py:102
  137.7 5.9 %fusion.75 = f32[128,72,96]{2,1,0:T(8,128)} fusion(bf16[72,72,128]{0,1,2:T(8,128)(2,1)} %copy.22, bf16[72,96,128]{1,0,2:T(8,128)(2,1)} %copy.23), kind=kOutput, calls=%fused_computation.121 | convolution fusion | flops 127401984 | bytes 6635520 | tf_op jit(solution)/shard_map/obc,oic->ibc/dot_general | solution.py:106
  143.6 5.7 %copy.24 = f32[128,72,96]{0,2,1:T(8,128)} copy(f32[128,72,96]{2,1,0:T(8,128)} %fusion.75) | data formatting | bytes 7077888 | tf_op jit(solution)/shard_map/obc,oic->ibc/dot_general | solution.py:106
  149.2 4.3 %bitcast_add_fusion = f32[72,96,128]{2,1,0:T(8,128)} fusion(f32[128,72,96]{0,2,1:T(8,128)} %copy.24, bf16[8,9,96,128]{3,2,1,0:T(8,128)(2,1)S(1)} %all-to-all-done), kind=kLoop, calls=%fused_computation.77 | loop fusion | flops 1769472 | bytes 8847360 | tf_op jit(solution)/shard_map/add | solution.py:107
  (48 shorter events, 11.6 us)
Async XLA Ops:
  1.8 3.0 %copy-start.3 = (f32[9]{0:T(128)S(1)}, f32[9]{0:T(128)}, u32[]{:S(2)}) copy-start(f32[9]{0:T(128)} %get-tuple-element.151) | copy-start | bytes 112 | tf_op jit(solution)/shard_map/while
  9.8 3.0 %copy-start.3 = (f32[9]{0:T(128)S(1)}, f32[9]{0:T(128)}, u32[]{:S(2)}) copy-start(f32[9]{0:T(128)} %get-tuple-element.151) | copy-start | bytes 112 | tf_op jit(solution)/shard_map/while
  17.8 3.0 %copy-start.3 = (f32[9]{0:T(128)S(1)}, f32[9]{0:T(128)}, u32[]{:S(2)}) copy-start(f32[9]{0:T(128)} %get-tuple-element.151) | copy-start | bytes 112 | tf_op jit(solution)/shard_map/while
  25.8 3.0 %copy-start.3 = (f32[9]{0:T(128)S(1)}, f32[9]{0:T(128)}, u32[]{:S(2)}) copy-start(f32[9]{0:T(128)} %get-tuple-element.151) | copy-start | bytes 112 | tf_op jit(solution)/shard_map/while
  33.8 3.0 %copy-start.3 = (f32[9]{0:T(128)S(1)}, f32[9]{0:T(128)}, u32[]{:S(2)}) copy-start(f32[9]{0:T(128)} %get-tuple-element.151) | copy-start | bytes 112 | tf_op jit(solution)/shard_map/while
  41.9 3.0 %copy-start.3 = (f32[9]{0:T(128)S(1)}, f32[9]{0:T(128)}, u32[]{:S(2)}) copy-start(f32[9]{0:T(128)} %get-tuple-element.151) | copy-start | bytes 112 | tf_op jit(solution)/shard_map/while
  49.9 3.0 %copy-start.3 = (f32[9]{0:T(128)S(1)}, f32[9]{0:T(128)}, u32[]{:S(2)}) copy-start(f32[9]{0:T(128)} %get-tuple-element.151) | copy-start | bytes 112 | tf_op jit(solution)/shard_map/while
  57.9 3.0 %copy-start.3 = (f32[9]{0:T(128)S(1)}, f32[9]{0:T(128)}, u32[]{:S(2)}) copy-start(f32[9]{0:T(128)} %get-tuple-element.151) | copy-start | bytes 112 | tf_op jit(solution)/shard_map/while
  65.9 3.0 %copy-start.3 = (f32[9]{0:T(128)S(1)}, f32[9]{0:T(128)}, u32[]{:S(2)}) copy-start(f32[9]{0:T(128)} %get-tuple-element.151) | copy-start | bytes 112 | tf_op jit(solution)/shard_map/while
  75.5 10.7 %copy-start.1 = (s32[2,1024]{1,0:T(2,128)S(1)}, s32[2,1024]{1,0:T(2,128)}, u32[]{:S(2)}) copy-start(s32[2,1024]{1,0:T(2,128)} %param.13) | copy-start | bytes 24580
  76.2 18.6 %collective-permute-start.1 = (f32[9,96,2,128]{3,2,1,0:T(2,128)S(1)}, f32[9,96,2,128]{3,2,1,0:T(2,128)S(1)}, u32[]{:S(2)}, u32[]{:S(2)}) collective-permute-start(f32[9,96,2,128]{3,2,1,0:T(2,128)S(1)} %get-tuple-element.87), channel_id=1, source_target_pairs={{1,0},{2,1},{3,2},{4,3},{5,4},{6,5},{7,6},{8,7},{9,8},{10,9},{11,1... | collective-permute-start | bytes 2654216 | tf_op jit(solution)/shard_map/ppermute | solution.py:21
  84.3 18.0 %collective-permute-start = (f32[9,96,2,128]{3,2,1,0:T(2,128)S(1)}, f32[9,96,2,128]{3,2,1,0:T(2,128)S(1)}, u32[]{:S(2)}, u32[]{:S(2)}) collective-permute-start(f32[9,96,2,128]{3,2,1,0:T(2,128)S(1)} %get-tuple-element.88), channel_id=1, source_target_pairs={{0,1},{1,2},{2,3},{3,4},{4,5},{5,6},{6,7},{7,8},{8,9},{9,10},{10,1... | collective-permute-start | bytes 2654216 | tf_op jit(solution)/shard_map/ppermute | solution.py:19
  86.3 0.9 copy-start
  112.9 8.2 %copy-start.2 = (s32[128]{0:T(128)S(1)}, s32[128]{0:T(128)}, u32[]{:S(2)}) copy-start(s32[128]{0:T(128)} %param.15) | copy-start | bytes 1540
  115.1 19.8 %all-to-all-start = ((bf16[8,9,96,128]{3,2,1,0:T(8,128)(2,1)}), bf16[8,9,96,128]{3,2,1,0:T(8,128)(2,1)S(1)}, u32[]{:S(2)}, u32[]{:S(2)}) async-start(bf16[8,9,96,128]{3,2,1,0:T(8,128)(2,1)} %fusion.60), calls=%async_computation | async-start | bytes 3538944 | tf_op jit(solution)/shard_map/all_to_all | solution.py:103
